TPU v7x, 32 devices: a whole 2x2x4 slice. The times are simulated.
32 devices in a mesh: grp: 2 (over x), blk: 16 (over z, y, core).
Axes of the slice: x: 2, y: 2, z: 4, core: 2. Of those that a mesh axis runs over, the one named last changes fastest.
Arguments:
- observed: bfloat16 [512, 16384], P(('grp', 'blk')), parts along dimension 0, may hold values from 0.03 to 2.1, as said below
- good_pixel_mask: int32 [512, 16384], P(('grp', 'blk')), parts along dimension 0, may hold values from 0 to 1, as said below
- templates: bfloat16 [512, 65632], P(('grp', 'blk')), parts along dimension 0, may hold values from -6 to 6
- template_kernel_index: int32 [512], P(('grp', 'blk')), parts along dimension 0, may hold values from 0 to 7
- line_spread_table: float32 [8, 97], replicated, may hold values from 0.05 to 1
- exposure_per_row: int32 [512], P('grp'), parts along dimension 0, may hold values from 0 to 255, each once
Outputs:
- ccf: float32 [512, 16384], P('grp', 'blk'), parts along dimension 0
There are 2 independent parts, one for each index of `grp`. A program takes and returns all parts, laid end to end along the dimension named above; an argument that names none is the same for every part. Nothing has to cross between parts.
Inputs may be any that keep to these rules, and one draw needn't show every extreme that they name: observed flux is positive, so masked is above zero exactly on good pixels. `good_pixel_mask`: some pixel columns are bad in every exposure.
All inputs are finite; a program needn't handle non-finite values.
Results may differ from a plain program's by a relative error of at most 0.0015.
Values may be sent and summed in bfloat16 or wider, within the bound.
A program may use at most 128 MiB of HBM per device.

v0:
```python
import functools
import math

import jax
import jax.numpy as jnp
from jax import lax
from jax.experimental import pallas as pl
from jax.experimental.pallas import tpu as pltpu
from jax.sharding import PartitionSpec as P

PIX = 16384
LAGS = 64
TAPS = 97
KERNELS = 8
Q = 128
R = PIX // Q
BAND = 640
F32 = jnp.float32
BF16 = jnp.bfloat16
NT_DIMS = (((1,), (1,)), ((), ()))


def template_kernel(index_ref, table_ref, templates_ref, x_ref, bands, chunks, smooth):
    count = templates_ref.shape[0]
    for k in range(KERNELS):
        row = jnp.broadcast_to(table_ref[k : k + 1, :], (Q, BAND))
        band = pltpu.roll(row, 0, 1, stride=4, stride_axis=0)
        high = band.astype(BF16)
        bands[k, :, :BAND] = high
        bands[k, :, BAND:] = (band - high.astype(F32)).astype(BF16)

    def spread(r, _):
        at = pl.multiple_of(r * (4 * Q), 128)
        piece = templates_ref[:, pl.ds(at, BAND)].astype(F32)
        for i in range(BAND // 128):
            chunks[i, pl.ds(pl.multiple_of(r * count, count), count), :] = piece[
                :, 128 * i : 128 * (i + 1)
            ]
        return 0

    lax.fori_loop(0, R - 1, spread, 0, unroll=8)
    last = (R - 1) * 4 * Q
    left = templates_ref.shape[1] - last
    tail = templates_ref[:, last:].astype(F32)
    tail = jnp.concatenate([tail, jnp.zeros((count, BAND - left), F32)], axis=1)
    for i in range(BAND // 128):
        chunks[i, (R - 1) * count :, :] = tail[:, 128 * i : 128 * (i + 1)]

    for t in range(count):
        rows = [
            chunks[i, pl.ds(t, R, stride=count), :].astype(BF16) for i in range(BAND // 128)
        ]
        rows = jnp.concatenate(rows + rows, axis=1)
        flux = lax.dot_general(
            bands[index_ref[t]], rows, NT_DIMS, preferred_element_type=F32
        )
        total = jnp.sum(flux * flux)
        smooth[pl.ds(t, Q, stride=count), :] = flux * lax.rsqrt(
            jnp.full((1, 1), total) / PIX + 1e-06
        )

    half = LAGS // 2
    body = smooth[...]
    lane = lax.broadcasted_iota(jnp.int32, (half * count, R), 1)
    x_ref[half * count : (half + Q) * count, :] = body.astype(BF16)
    before = pltpu.roll(body[(Q - half) * count :, :], 1, 1)
    x_ref[: half * count, :] = jnp.where(lane == 0, 0.0, before).astype(BF16)
    after = pltpu.roll(body[: half * count, :], R - 1, 1)
    x_ref[(half + Q) * count :, :] = jnp.where(lane == R - 1, 0.0, after).astype(BF16)


def shape_templates(templates, template_kernel_index, line_spread_table):
    count = templates.shape[0]
    table = jnp.pad(line_spread_table, ((0, 0), (0, BAND - TAPS)))
    return pl.pallas_call(
        template_kernel,
        out_shape=jax.ShapeDtypeStruct(((Q + LAGS) * count, R), BF16),
        in_specs=[
            pl.BlockSpec(memory_space=pltpu.SMEM),
            pl.BlockSpec(memory_space=pltpu.VMEM),
            pl.BlockSpec(memory_space=pltpu.VMEM),
        ],
        out_specs=pl.BlockSpec(memory_space=pltpu.VMEM),
        scratch_shapes=[
            pltpu.VMEM((KERNELS, Q, 2 * BAND), BF16),
            pltpu.VMEM((BAND // 128, R * count, 128), F32),
            pltpu.VMEM((Q * count, R), F32),
        ],
        compiler_params=pltpu.CompilerParams(vmem_limit_bytes=40 * 2**20),
        cost_estimate=pl.CostEstimate(
            flops=2 * count * Q * R * 2 * BAND, bytes_accessed=6 * 2**20, transcendentals=0
        ),
        name="shape_templates",
    )(template_kernel_index, table, templates)


def correlate_kernel(step_q, rows_ref, x_ref, g_ref, out_ref, acc):
    step = pl.program_id(0)
    total_rows = rows_ref.shape[1]
    count = x_ref.shape[0] // (Q + LAGS)
    tile = 256

    @pl.when(step == 0)
    def _():
        acc[...] = jnp.zeros_like(acc)

    right = jnp.concatenate([g_ref[i] for i in range(step_q)], axis=1)
    for m in range(LAGS * count // tile):
        left = jnp.concatenate(
            [
                x_ref[pl.ds(pl.multiple_of((step * step_q + i) * count + m * tile, 16), tile), :]
                for i in range(step_q)
            ],
            axis=1,
        )
        part = lax.dot_general(left, right, NT_DIMS, preferred_element_type=F32)
        for h in range(total_rows // 128):
            acc[h, m * tile : (m + 1) * tile, :] += part[:, 128 * h : 128 * (h + 1)]

    @pl.when(step == pl.num_programs(0) - 1)
    def _():
        place = (
            lax.broadcasted_iota(jnp.int32, (total_rows, total_rows), 0) == rows_ref[...]
        ).astype(BF16)
        both = jnp.concatenate([place, place], axis=1)
        for t in range(0, count, 2):
            part = jnp.concatenate(
                [
                    jnp.concatenate(
                        [
                            acc[h, pl.ds(t + i, LAGS, stride=count), :]
                            for h in range(total_rows // 128)
                        ],
                        axis=1,
                    )
                    for i in range(2)
                ],
                axis=0,
            ) * F32(1.0 / math.sqrt(PIX))
            high = part.astype(BF16)
            low = (part - high.astype(F32)).astype(BF16)
            out_ref[:, t * LAGS : (t + 2) * LAGS] = lax.dot_general(
                both,
                jnp.concatenate([high, low], axis=1),
                NT_DIMS,
                preferred_element_type=F32,
            )


def correlate(x, gathered, exposure_per_row):
    total_rows = gathered.shape[1]
    count = x.shape[0] // (Q + LAGS)
    step_q = 8
    return pl.pallas_call(
        functools.partial(correlate_kernel, step_q),
        grid=(Q // step_q,),
        out_shape=jax.ShapeDtypeStruct((total_rows, count * LAGS), F32),
        in_specs=[
            pl.BlockSpec((1, total_rows), lambda s: (0, 0)),
            pl.BlockSpec(x.shape, lambda s: (0, 0)),
            pl.BlockSpec((step_q, total_rows, R), lambda s: (s, 0, 0)),
        ],
        out_specs=pl.BlockSpec((total_rows, count * LAGS), lambda s: (0, 0)),
        scratch_shapes=[pltpu.VMEM((total_rows // 128, LAGS * count, 128), F32)],
        compiler_params=pltpu.CompilerParams(vmem_limit_bytes=40 * 2**20),
        name="correlate",
    )(exposure_per_row.reshape(1, total_rows), x, gathered)


def shards(
    observed, good_pixel_mask, templates, template_kernel_index, line_spread_table, exposure_per_row
):
    rows = observed.shape[0]
    x = shape_templates(templates, template_kernel_index, line_spread_table)
    good = good_pixel_mask > 0
    flux = jnp.where(good, observed, 0).astype(F32)
    present = (flux > 0).astype(F32)
    sums = lax.psum(jnp.stack([jnp.sum(flux, axis=0), jnp.sum(present, axis=0)]), "blk")
    mean = sums[0] / jnp.maximum(sums[1], 1.0)
    resid = present * (flux - mean[None, :])
    scale = lax.rsqrt(jnp.sum(resid * resid, axis=1) / PIX + 1e-06)
    ready = (resid * scale[:, None]).astype(BF16)
    ready = ready.reshape(rows, R, Q).transpose(2, 0, 1)
    gathered = lax.all_gather(ready, "blk", axis=1, tiled=True)
    return correlate(x, gathered, exposure_per_row)


def solution(mesh):
    in_specs = (
        P(("grp", "blk"), None),
        P(("grp", "blk"), None),
        P(("grp", "blk"), None),
        P(("grp", "blk")),
        P(),
        P("grp"),
    )
    out_specs = P("grp", "blk")
    return jax.shard_map(shards, mesh=mesh, in_specs=in_specs, out_specs=out_specs, check_vma=False)
```

profile of v0, /device:TPU:0, one launch (start us, length us, event | category | flops | bytes accessed | tf_op | source)
XLA Modules:
  0.0 207.8 jit_solution(7838464625733429726)
XLA Ops:
  6.5 0.0 copy-start.2
  6.5 0.0 all-reduce.3.cloned.1.call-start
  6.5 1.9 convert_reduce_fusion
  8.4 0.8 pad_maximum_fusion
  9.2 0.0 all-reduce.3.cloned.1.call-update
  9.2 0.0 all-gather.2.cloned.1.call-start
  9.3 91.3 %all-reduce.3.cloned.1.call-done = f32[2,16384]{1,0:T(2,128)} async-done(((f32[2,16384]{1,0:T(2,128)}), f32[2,16384]{1,0:T(2,128)}) %all-reduce.3.cloned.1.call-update) | async-done | bytes 131088 | tf_op jit(solution)/shard_map/psum | solution.py:178
  100.5 1.1 fusion.8
  101.6 0.3 fusion.5
  101.9 0.3 fusion.7
  102.2 0.1 copy.8
  102.3 1.2 copy.7
  103.5 0.0 all-gather.2.cloned.1.call-update
  103.5 0.7 pad.4.table_ref
  104.2 0.0 copy-start.1
  104.2 1.6 copy-done.1
  105.8 0.0 copy-start.3
  105.8 0.7 copy-done.3
  106.5 4.3 %shape_templates.1.x_ref = bf16[3072,128]{1,0:T(8,128)(2,1)S(1)} custom-call(s32[16]{0:T(128)S(1)} %copy-done.3, f32[8,640]{1,0:T(8,128)S(1)} %pad.4.table_ref, bf16[16,65632]{1,0:T(8,128)(2,1)S(1)} %copy-done.1), custom_call_target="tpu_custom_call" | custom-call | flops 671088640 | bytes 6291456 | tf_op jit(solution)/shard_map/shape_templates/pallas_call | solution.py:75
  110.8 72.7 %all-gather.2.cloned.1.call-done.g_ref = bf16[128,256,128]{2,1,0:T(8,128)(2,1)} async-done(((bf16[128,16,128]{2,1,0:T(8,128)(2,1)}), bf16[128,256,128]{2,1,0:T(8,128)(2,1)}) %all-gather.2.cloned.1.call-update) | async-done | bytes 8388624 | tf_op jit(solution)/shard_map/all_gather | solution.py:184
  183.4 0.0 copy-done.2
  183.4 0.0 copy-start
  183.4 3.4 %copy-done = bf16[128,256,128]{2,1,0:T(8,128)(2,1)S(1)} copy-done((bf16[128,256,128]{2,1,0:T(8,128)(2,1)S(1)}, bf16[128,256,128]{2,1,0:T(8,128)(2,1)}, u32[]{:S(2)}) %copy-start) | copy-done | bytes 8388632
  186.8 14.1 %correlate.1 = f32[256,1024]{1,0:T(8,128)} custom-call(s32[1,256]{1,0:T(1,128)S(1)} %bitcast.8, bf16[3072,128]{1,0:T(8,128)(2,1)S(1)} %shape_templates.1.x_ref, bf16[128,256,128]{2,1,0:T(8,128)(2,1)S(1)} %copy-done), custom_call_target="tpu_custom_call" | custom-call | tf_op jit(solution)/shard_map/correlate/pallas_call | solution.py:154
  (1 shorter events, 0.0 us)
Async XLA Ops:
  6.5 176.9 %copy-start.2 = (s32[256]{0:T(256)S(1)}, s32[256]{0:T(256)}, u32[]{:S(2)}) copy-start(s32[256]{0:T(256)} %param.11) | copy-start | bytes 3076
  6.5 94.0 %all-reduce.3.cloned.1.call-start = ((), (), s32[]{:S(2)}) async-start(), calls=%async_computation | async-start | bytes 262144 | tf_op jit(solution)/shard_map/psum | solution.py:178
  9.2 174.2 %all-gather.2.cloned.1.call-start = ((), (), s32[]{:S(2)}) async-start(), calls=%async_computation.1 | async-start | bytes 8912896 | tf_op jit(solution)/shard_map/all_gather | solution.py:184
  104.2 1.6 copy-start.1
  105.8 0.7 copy-start.3
  183.4 3.4 %copy-start = (bf16[128,256,128]{2,1,0:T(8,128)(2,1)S(1)}, bf16[128,256,128]{2,1,0:T(8,128)(2,1)}, u32[]{:S(2)}) copy-start(bf16[128,256,128]{2,1,0:T(8,128)(2,1)} %all-gather.2.cloned.1.call-done.g_ref) | copy-start | bytes 25165828
Sparse Core Ops, SparseCore 0:
  10.8 89.6 all-reduce.2
  103.7 79.7 all-gather.1
where the time goes:
time: 208 us
  waiting for transfers between devices  164 us (79%)
  Pallas kernels  18.4 us (9%)
  between operations  13.4 us (6%)
  local copies, waits for them, and re-layouts  7.63 us (4%)
  other arithmetic  4.31 us (2%)
    psum x1, waiting for transfers between devices, shards(): lax.psum(jnp.stack([jnp.sum(flux, axis=0), jnp.sum(present, axis=0)]), 'b...  91.3 us
    all_gather x1, waiting for transfers between devices, shards(): gathered = lax.all_gather(ready, 'blk', axis=1, tiled=True)  72.7 us
    pallas_call x1, Pallas kernels, correlate(): pl.pallas_call(functools.partial(correlate_kernel, step_q), grid=(Q // st...  14.1 us
    unnamed x9, local copies, waits for them, and re-layouts  5.72 us
    pallas_call x1, Pallas kernels, shape_templates(): pl.pallas_call(template_kernel, out_shape=jax.ShapeDtypeStruct(((Q + LAGS...  4.27 us
  transfers between devices with their start and end apart: 2, of which 2 were waited for; matrix products, arithmetic and copies ran while one was open for 0% of the time, Pallas kernels for 2%

commit v1 on v0

--- a/solution.py
+++ b/solution.py
@@ -17,6 +17,7 @@
 BAND = 640
 F32 = jnp.float32
 BF16 = jnp.bfloat16
+MESH = pl.DeviceIdType.MESH
 NT_DIMS = (((1,), (1,)), ((), ()))
 
 
@@ -94,6 +95,36 @@
     )(template_kernel_index, table, templates)
 
 
+def place_rows(rows_ref, acc, out_ref, count):
+    total_rows = rows_ref.shape[1]
+    chosen = (
+        lax.broadcasted_iota(jnp.int32, (total_rows, total_rows), 0) == rows_ref[...]
+    ).astype(BF16)
+    both = jnp.concatenate([chosen, chosen], axis=1)
+    for t in range(0, count, 2):
+        part = jnp.concatenate(
+            [
+                jnp.concatenate(
+                    [
+                        acc[h, pl.ds(t + i, LAGS, stride=count), :]
+                        for h in range(total_rows // 128)
+                    ],
+                    axis=1,
+                )
+                for i in range(2)
+            ],
+            axis=0,
+        ) * F32(1.0 / math.sqrt(PIX))
+        high = part.astype(BF16)
+        low = (part - high.astype(F32)).astype(BF16)
+        out_ref[:, t * LAGS : (t + 2) * LAGS] = lax.dot_general(
+            both,
+            jnp.concatenate([high, low], axis=1),
+            NT_DIMS,
+            preferred_element_type=F32,
+        )
+
+
 def correlate_kernel(step_q, rows_ref, x_ref, g_ref, out_ref, acc):
     step = pl.program_id(0)
     total_rows = rows_ref.shape[1]
@@ -119,32 +150,7 @@
 
     @pl.when(step == pl.num_programs(0) - 1)
     def _():
-        place = (
-            lax.broadcasted_iota(jnp.int32, (total_rows, total_rows), 0) == rows_ref[...]
-        ).astype(BF16)
-        both = jnp.concatenate([place, place], axis=1)
-        for t in range(0, count, 2):
-            part = jnp.concatenate(
-                [
-                    jnp.concatenate(
-                        [
-                            acc[h, pl.ds(t + i, LAGS, stride=count), :]
-                            for h in range(total_rows // 128)
-                        ],
-                        axis=1,
-                    )
-                    for i in range(2)
-                ],
-                axis=0,
-            ) * F32(1.0 / math.sqrt(PIX))
-            high = part.astype(BF16)
-            low = (part - high.astype(F32)).astype(BF16)
-            out_ref[:, t * LAGS : (t + 2) * LAGS] = lax.dot_general(
-                both,
-                jnp.concatenate([high, low], axis=1),
-                NT_DIMS,
-                preferred_element_type=F32,
-            )
+        place_rows(rows_ref, acc, out_ref, count)
 
 
 def correlate(x, gathered, exposure_per_row):
@@ -167,20 +173,281 @@
     )(exposure_per_row.reshape(1, total_rows), x, gathered)
 
 
+def mean_kernel(n, part_ref, mean_ref, slots, own_mean, send_sem, recv_sem):
+    me = lax.axis_index("blk")
+    barrier = pltpu.get_barrier_semaphore()
+
+    def greet(o, _):
+        pl.semaphore_signal(
+            barrier, inc=1, device_id={"blk": lax.rem(me + o, n)}, device_id_type=MESH
+        )
+        return 0
+
+    lax.fori_loop(1, n, greet, 0)
+    pl.semaphore_wait(barrier, n - 1)
+
+    def part_copy(o):
+        to = lax.rem(me + o, n)
+        return pltpu.make_async_remote_copy(
+            src_ref=part_ref.at[to],
+            dst_ref=slots.at[o],
+            send_sem=send_sem.at[0, o],
+            recv_sem=recv_sem.at[0, o],
+            device_id={"blk": to},
+            device_id_type=MESH,
+        )
+
+    def mean_copy(o):
+        return pltpu.make_async_remote_copy(
+            src_ref=own_mean,
+            dst_ref=mean_ref.at[me],
+            send_sem=send_sem.at[1, o],
+            recv_sem=recv_sem.at[1, o],
+            device_id={"blk": lax.rem(me + o, n)},
+            device_id_type=MESH,
+        )
+
+    for o in range(1, n):
+        part_copy(o).start()
+    total = part_ref[me]
+    for o in range(1, n):
+        part_copy(o).wait_recv()
+        total = total + slots[o]
+    own_mean[...] = total[0] / jnp.maximum(total[1], 1.0)
+    for o in range(1, n):
+        mean_copy(o).start()
+    mean_ref[me] = own_mean[...]
+    for o in range(1, n):
+        mean_copy(o).wait_recv()
+    for o in range(1, n):
+        part_copy(o).wait_send()
+        mean_copy(o).wait_send()
+
+
+def column_means(sums, counts, n):
+    part = jnp.stack([sums.reshape(n, -1, 128), counts.reshape(n, -1, 128)], axis=1)
+    share = part.shape[2]
+    mean = pl.pallas_call(
+        functools.partial(mean_kernel, n),
+        out_shape=jax.ShapeDtypeStruct((n, share, 128), F32),
+        in_specs=[pl.BlockSpec(memory_space=pltpu.VMEM)],
+        out_specs=pl.BlockSpec(memory_space=pltpu.VMEM),
+        scratch_shapes=[
+            pltpu.VMEM((n, 2, share, 128), F32),
+            pltpu.VMEM((share, 128), F32),
+            pltpu.SemaphoreType.DMA((2, n)),
+            pltpu.SemaphoreType.DMA((2, n)),
+        ],
+        compiler_params=pltpu.CompilerParams(collective_id=0, has_side_effects=True),
+        name="column_means",
+    )(part)
+    return mean.reshape(-1)
+
+
+def gather_kernel(chunks, ready_ref, x_ref, acc_ref, held, send_sem, recv_sem):
+    me = lax.axis_index("blk")
+    z, y, c = me // 4, (me // 2) % 2, me % 2
+    span = Q // chunks
+    count = x_ref.shape[0] // (Q + LAGS)
+    rows = ready_ref.shape[1]
+    planes, total_rows = 4, 16 * rows
+    tile = 256
+
+    def blk(zz, yy, cc):
+        return (zz * 2 + yy) * 2 + cc
+
+    up, down = blk(z + 1, y, c), blk(z - 1, y, c)
+    beside, twin = blk(z, 1 - y, c), blk(z, y, 1 - c)
+
+    barrier = pltpu.get_barrier_semaphore()
+
+    def greet(to):
+        pl.semaphore_signal(barrier, inc=1, device_id={"blk": to}, device_id_type=MESH)
+
+    greet(beside)
+    greet(twin)
+    pl.when(z < planes - 1)(lambda: greet(up))
+    pl.when(z > 0)(lambda: greet(down))
+    held[me] = ready_ref[...]
+    acc_ref[...] = jnp.zeros_like(acc_ref)
+    inner = (z > 0).astype(jnp.int32) + (z < planes - 1).astype(jnp.int32)
+    pl.semaphore_wait(barrier, 2 + inner)
+
+    def copy(source, k, slot, to):
+        part = held.at[source, pl.ds(k * span, span)]
+        return pltpu.make_async_remote_copy(
+            src_ref=part,
+            dst_ref=part,
+            send_sem=send_sem.at[slot, k],
+            recv_sem=recv_sem.at[source, k],
+            device_id={"blk": to},
+            device_id_type=MESH,
+        )
+
+    def z_part(h, k, sign, finish):
+        zs = z - sign * h
+        source = blk(zs, y, c)
+
+        def go():
+            if h > 0 and not finish:
+                copy(source, k, 0, twin).wait_recv()
+
+            def act(slot, to):
+                one = copy(source, k, slot, to)
+                if finish:
+                    one.wait_send()
+                else:
+                    one.start()
+
+            act(8 + zs, beside)
+            if sign > 0 or h == 0:
+                pl.when(z < planes - 1)(lambda: act(zs, up))
+            if sign < 0 or h == 0:
+                pl.when(z > 0)(lambda: act(4 + zs, down))
+            act(12 + zs, twin)
+
+        if h == 0:
+            go()
+        else:
+            pl.when((zs >= 0) & (zs < planes))(go)
+
+    def y_part(h, k, sign, finish):
+        zs = z - sign * h
+        source = blk(zs, 1 - y, c)
+
+        def go():
+            one = copy(source, k, 16 + zs, twin)
+            if finish:
+                one.wait_send()
+            else:
+                one.wait_recv()
+                one.start()
+
+        if h == 0:
+            go()
+        else:
+            pl.when((zs >= 0) & (zs < planes))(go)
+
+    def each_hop(part, k_of, finish):
+        for h in range(planes):
+            k = k_of(h)
+
+            @pl.when((k >= 0) & (k < chunks))
+            def _():
+                part(h, k, 1, finish)
+                if h > 0:
+                    part(h, k, -1, finish)
+
+    def product(k):
+        for zy in range(2 * planes):
+            copy(zy * 2 + 1 - c, k, 0, twin).wait_recv()
+        right = jnp.concatenate(
+            [held[:, k * span + i].reshape(total_rows, R) for i in range(span)], axis=1
+        )
+
+        def one_tile(m, _):
+            left = jnp.concatenate(
+                [
+                    x_ref[pl.ds(pl.multiple_of((k * span + i) * count + m * tile, 16), tile), :]
+                    for i in range(span)
+                ],
+                axis=1,
+            )
+            acc_ref[pl.ds(pl.multiple_of(m * tile, tile), tile), :] += lax.dot_general(
+                left, right, NT_DIMS, preferred_element_type=F32
+            )
+            return 0
+
+        for m in range(LAGS * count // tile):
+            one_tile(m, 0)
+
+    lag = planes + 1
+
+    def step(s, _):
+        each_hop(z_part, lambda h: s - h, False)
+        each_hop(y_part, lambda h: s - h - 1, False)
+        pl.when(s >= lag)(lambda: product(s - lag))
+        return 0
+
+    lax.fori_loop(0, chunks + lag, step, 0)
+
+    def finish(k, _):
+        each_hop(z_part, lambda h: k, True)
+        each_hop(y_part, lambda h: k, True)
+        return 0
+
+    lax.fori_loop(0, chunks, finish, 0)
+
+
+def gather_correlate(x, ready):
+    rows = ready.shape[1]
+    count = x.shape[0] // (Q + LAGS)
+    chunks = 8
+    return pl.pallas_call(
+        functools.partial(gather_kernel, chunks),
+        out_shape=jax.ShapeDtypeStruct((LAGS * count, 16 * rows), F32),
+        in_specs=[pl.BlockSpec(memory_space=pltpu.VMEM)] * 2,
+        out_specs=pl.BlockSpec(memory_space=pltpu.VMEM),
+        scratch_shapes=[
+            pltpu.VMEM((16, Q, rows, R), BF16),
+            pltpu.SemaphoreType.DMA((20, chunks)),
+            pltpu.SemaphoreType.DMA((16, chunks)),
+        ],
+        compiler_params=pltpu.CompilerParams(
+            collective_id=1, has_side_effects=True, vmem_limit_bytes=40 * 2**20
+        ),
+        name="gather_correlate",
+    )(ready, x)
+
+
+def place_kernel(rows_ref, acc_ref, out_ref, split):
+    total_rows = rows_ref.shape[1]
+    count = acc_ref.shape[0] // LAGS
+    for h in range(total_rows // 128):
+        split[h] = acc_ref[:, 128 * h : 128 * (h + 1)]
+    place_rows(rows_ref, split, out_ref, count)
+
+
+def place(acc, exposure_per_row):
+    total_rows = acc.shape[1]
+    return pl.pallas_call(
+        place_kernel,
+        out_shape=jax.ShapeDtypeStruct((total_rows, acc.shape[0]), F32),
+        in_specs=[pl.BlockSpec(memory_space=pltpu.VMEM)] * 2,
+        out_specs=pl.BlockSpec(memory_space=pltpu.VMEM),
+        scratch_shapes=[pltpu.VMEM((total_rows // 128, acc.shape[0], 128), F32)],
+        compiler_params=pltpu.CompilerParams(vmem_limit_bytes=16 * 2**20),
+        name="place",
+    )(exposure_per_row.reshape(1, total_rows), acc)
+
+
 def shards(
-    observed, good_pixel_mask, templates, template_kernel_index, line_spread_table, exposure_per_row
+    devices,
+    observed,
+    good_pixel_mask,
+    templates,
+    template_kernel_index,
+    line_spread_table,
+    exposure_per_row,
 ):
     rows = observed.shape[0]
+    ring = devices == 16 and rows % 16 == 0
     x = shape_templates(templates, template_kernel_index, line_spread_table)
     good = good_pixel_mask > 0
     flux = jnp.where(good, observed, 0).astype(F32)
     present = (flux > 0).astype(F32)
-    sums = lax.psum(jnp.stack([jnp.sum(flux, axis=0), jnp.sum(present, axis=0)]), "blk")
-    mean = sums[0] / jnp.maximum(sums[1], 1.0)
+    sums, counts = jnp.sum(flux, axis=0), jnp.sum(present, axis=0)
+    if ring:
+        mean = column_means(sums, counts, devices)
+    else:
+        sums = lax.psum(jnp.stack([sums, counts]), "blk")
+        mean = sums[0] / jnp.maximum(sums[1], 1.0)
     resid = present * (flux - mean[None, :])
     scale = lax.rsqrt(jnp.sum(resid * resid, axis=1) / PIX + 1e-06)
     ready = (resid * scale[:, None]).astype(BF16)
     ready = ready.reshape(rows, R, Q).transpose(2, 0, 1)
+    if ring:
+        return place(gather_correlate(x, ready), exposure_per_row)
     gathered = lax.all_gather(ready, "blk", axis=1, tiled=True)
     return correlate(x, gathered, exposure_per_row)
 
@@ -195,4 +462,10 @@
         P("grp"),
     )
     out_specs = P("grp", "blk")
-    return jax.shard_map(shards, mesh=mesh, in_specs=in_specs, out_specs=out_specs, check_vma=False)
+    return jax.shard_map(
+        functools.partial(shards, mesh.shape["blk"]),
+        mesh=mesh,
+        in_specs=in_specs,
+        out_specs=out_specs,
+        check_vma=False,
+    )

time: 208 us -> 87.7 us (0.42)
  waiting for transfers between devices: 164 us -> 0 us
  Pallas kernels: 18.4 us -> 81.3 us
  between operations: 13.4 us -> 0.1 us
  local copies, waits for them, and re-layouts: 7.63 us -> 1.24 us
    psum x1 -> x0, waiting for transfers between devices: 91.3 us -> none  [shards(): lax.psum(jnp.stack([jnp.sum(flux, axis=0), jnp.sum(present, axis=0)]), 'b...]
    all_gather x1 -> x0, waiting for transfers between devices: 72.7 us -> none  [shards(): gathered = lax.all_gather(ready, 'blk', axis=1, tiled=True)]
    pallas_call x1 -> x3, Pallas kernels: 14.1 us -> 77 us  [the longest x1 57.6 us: gather_correlate(): pl.pallas_call(functools.partial(gather_kernel, chunks), out_shape=jax.Sh...]
    unnamed x9 -> x7, local copies, waits for them, and re-layouts: 5.72 us -> 0.11 us
  transfers between devices with their start and end apart: 2 -> 0, of which waited for: 2 -> 0; matrix products, arithmetic and copies ran while one was open for 0% -> 0% of each run, Pallas kernels for 2% -> 0%
where the time goes in v1:
time: 87.7 us; the launch traced here: 87.4 us
  Pallas kernels  81.3 us (93%)
  other arithmetic  4.79 us (5%)
  local copies, waits for them, and re-layouts  1.24 us (1%)
    pallas_call x1, Pallas kernels, gather_correlate(): pl.pallas_call(functools.partial(gather_kernel, chunks), out_shape=jax.Sh...  57.6 us
    pallas_call x1, Pallas kernels, column_means(): pl.pallas_call(functools.partial(mean_kernel, n), out_shape=jax.ShapeDtyp...  17.5 us
    pallas_call x1, Pallas kernels, shape_templates(): pl.pallas_call(template_kernel, out_shape=jax.ShapeDtypeStruct(((Q + LAGS...  4.3 us
    pallas_call x1, Pallas kernels, place(): pl.pallas_call(place_kernel, out_shape=jax.ShapeDtypeStruct((total_rows,...  1.86 us
    reduce_sum x1, other arithmetic, shards(): sums, counts = (jnp.sum(flux, axis=0), jnp.sum(present, axis=0))  1.86 us

profile of v1, /device:TPU:0, one launch (start us, length us, event | category | flops | bytes accessed | tf_op | source)
XLA Modules:
  0.0 87.4 jit_solution(9560176951472188828)
XLA Ops:
  0.0 0.7 pad.4.table_ref
  0.7 1.9 %convert_reduce_fusion = (f32[16384]{0:T(1024)S(1)}, f32[16384]{0:T(1024)S(1)}, bf16[16,16384]{1,0:T(8,128)(2,1)S(1)}) fusion(bf16[16,16384]{1,0:T(8,128)(2,1)} %param.6, s32[16,16384]{1,0:T(8,128)} %param.7), kind=kLoop, calls=%fused_computation.1 | loop fusion | flops 1802240 | bytes 2228224 | tf_op jit(solution)/shard_map/reduce_sum | solution.py:439
  2.6 0.0 copy-start
  2.6 0.0 copy-start.2
  2.6 0.7 pad_maximum_fusion.part_ref
  3.2 17.5 %column_means.1 = f32[16,8,128]{2,1,0:T(8,128)} custom-call(f32[16,2,8,128]{3,2,1,0:T(8,128)} %pad_maximum_fusion.part_ref), custom_call_target="tpu_custom_call" | custom-call | tf_op jit(solution)/shard_map/column_means/pallas_call | solution.py:230
  20.8 1.2 %fusion.5 = f32[16]{0:T(128)S(1)} fusion(bf16[16,16384]{1,0:T(8,128)(2,1)S(1)} %get-tuple-element.7, f32[16384]{0:T(1024)} %bitcast.11), kind=kLoop, calls=%fused_computation.8 | loop fusion | flops 1572848 | bytes 589888 | tf_op jit(solution)/shard_map/reduce_sum | solution.py:446
  21.9 1.1 %fusion.7 = bf16[2,8,128,128]{3,1,2,0:T(8,128)(2,1)S(1)} fusion(bf16[16,16384]{1,0:T(8,128)(2,1)S(1)} %get-tuple-element.7, f32[16]{0:T(128)S(1)} %add_rsqrt_fusion, f32[16384]{0:T(1024)} %bitcast.12), kind=kLoop, calls=%fused_computation.11 | loop fusion | flops 1572864 | bytes 1114176
  23.0 0.1 copy.8
  23.1 0.4 copy.7
  23.6 0.0 copy-done
  23.6 0.0 copy-done.2
  23.6 0.0 copy-start.1
  23.6 4.3 %shape_templates.1.x_ref = bf16[3072,128]{1,0:T(8,128)(2,1)S(1)} custom-call(s32[16]{0:T(128)S(1)} %copy-done.2, f32[8,640]{1,0:T(8,128)S(1)} %pad.4.table_ref, bf16[16,65632]{1,0:T(8,128)(2,1)S(1)} %copy-done), custom_call_target="tpu_custom_call" | custom-call | flops 671088640 | bytes 6291456 | tf_op jit(solution)/shard_map/shape_templates/pallas_call | solution.py:76
  27.9 57.6 %gather_correlate.1.acc_ref = f32[1024,256]{1,0:T(8,128)S(1)} custom-call(bf16[128,16,128]{2,1,0:T(8,128)(2,1)S(1)} %bitcast.8, bf16[3072,128]{1,0:T(8,128)(2,1)S(1)} %shape_templates.1.x_ref), custom_call_target="tpu_custom_call" | custom-call | tf_op jit(solution)/shard_map/gather_correlate/pallas_call | solution.py:386
  85.6 0.0 copy-done.1
  85.6 1.9 %place.1 = f32[256,1024]{1,0:T(8,128)} custom-call(s32[1,256]{1,0:T(1,128)S(1)} %bitcast.9, f32[1024,256]{1,0:T(8,128)S(1)} %gather_correlate.1.acc_ref), custom_call_target="tpu_custom_call" | custom-call | tf_op jit(solution)/shard_map/place/pallas_call | solution.py:413
  (1 shorter events, 0.0 us)
Async XLA Ops:
  2.6 21.0 %copy-start = (bf16[16,65632]{1,0:T(8,128)(2,1)S(1)}, bf16[16,65632]{1,0:T(8,128)(2,1)}, u32[]{:S(2)}) copy-start(bf16[16,65632]{1,0:T(8,128)(2,1)} %templates_ref.1) | copy-start | bytes 6300676
  2.6 21.0 %copy-start.2 = (s32[16]{0:T(128)S(1)}, s32[16]{0:T(128)}, u32[]{:S(2)}) copy-start(s32[16]{0:T(128)} %index_ref.1) | copy-start | bytes 196
  23.6 62.0 %copy-start.1 = (s32[256]{0:T(256)S(1)}, s32[256]{0:T(256)}, u32[]{:S(2)}) copy-start(s32[256]{0:T(256)} %param.11) | copy-start | bytes 3076

commit v2 on v1

--- a/solution.py
+++ b/solution.py
@@ -15,6 +15,8 @@
 Q = 128
 R = PIX // Q
 BAND = 640
+CHUNKS = 8
+AHEAD = 1
 F32 = jnp.float32
 BF16 = jnp.bfloat16
 MESH = pl.DeviceIdType.MESH
@@ -22,6 +24,13 @@
 
 
 def template_kernel(index_ref, table_ref, templates_ref, x_ref, bands, chunks, smooth):
+    count = templates_ref.shape[0]
+    spread_templates(table_ref, templates_ref, bands, chunks)
+    smooth_templates(index_ref, bands, chunks, smooth, 0, count, count)
+    pack_templates(smooth, x_ref, count)
+
+
+def spread_templates(table_ref, templates_ref, bands, chunks):
     count = templates_ref.shape[0]
     for k in range(KERNELS):
         row = jnp.broadcast_to(table_ref[k : k + 1, :], (Q, BAND))
@@ -47,7 +56,9 @@
     for i in range(BAND // 128):
         chunks[i, (R - 1) * count :, :] = tail[:, 128 * i : 128 * (i + 1)]
 
-    for t in range(count):
+
+def smooth_templates(index_ref, bands, chunks, smooth, first, last, count):
+    for t in range(first, last):
         rows = [
             chunks[i, pl.ds(t, R, stride=count), :].astype(BF16) for i in range(BAND // 128)
         ]
@@ -60,6 +71,8 @@
             jnp.full((1, 1), total) / PIX + 1e-06
         )
 
+
+def pack_templates(smooth, x_ref, count):
     half = LAGS // 2
     body = smooth[...]
     lane = lax.broadcasted_iota(jnp.int32, (half * count, R), 1)
@@ -173,7 +186,23 @@
     )(exposure_per_row.reshape(1, total_rows), x, gathered)
 
 
-def mean_kernel(n, part_ref, mean_ref, slots, own_mean, send_sem, recv_sem):
+def mean_kernel(
+    n,
+    part_ref,
+    index_ref,
+    table_ref,
+    templates_ref,
+    mean_ref,
+    x_ref,
+    slots,
+    own_mean,
+    send_sem,
+    recv_sem,
+    bands,
+    chunks,
+    smooth,
+):
+    count = templates_ref.shape[0]
     me = lax.axis_index("blk")
     barrier = pltpu.get_barrier_semaphore()
 
@@ -209,6 +238,8 @@
 
     for o in range(1, n):
         part_copy(o).start()
+    spread_templates(table_ref, templates_ref, bands, chunks)
+    smooth_templates(index_ref, bands, chunks, smooth, 0, count // 2, count)
     total = part_ref[me]
     for o in range(1, n):
         part_copy(o).wait_recv()
@@ -217,6 +248,8 @@
     for o in range(1, n):
         mean_copy(o).start()
     mean_ref[me] = own_mean[...]
+    smooth_templates(index_ref, bands, chunks, smooth, count // 2, count, count)
+    pack_templates(smooth, x_ref, count)
     for o in range(1, n):
         mean_copy(o).wait_recv()
     for o in range(1, n):
@@ -224,24 +257,39 @@
         mean_copy(o).wait_send()
 
 
-def column_means(sums, counts, n):
+def column_means(sums, counts, n, templates, template_kernel_index, line_spread_table):
     part = jnp.stack([sums.reshape(n, -1, 128), counts.reshape(n, -1, 128)], axis=1)
     share = part.shape[2]
-    mean = pl.pallas_call(
+    count = templates.shape[0]
+    table = jnp.pad(line_spread_table, ((0, 0), (0, BAND - TAPS)))
+    mean, x = pl.pallas_call(
         functools.partial(mean_kernel, n),
-        out_shape=jax.ShapeDtypeStruct((n, share, 128), F32),
-        in_specs=[pl.BlockSpec(memory_space=pltpu.VMEM)],
-        out_specs=pl.BlockSpec(memory_space=pltpu.VMEM),
+        out_shape=(
+            jax.ShapeDtypeStruct((n, share, 128), F32),
+            jax.ShapeDtypeStruct(((Q + LAGS) * count, R), BF16),
+        ),
+        in_specs=[
+            pl.BlockSpec(memory_space=pltpu.VMEM),
+            pl.BlockSpec(memory_space=pltpu.SMEM),
+            pl.BlockSpec(memory_space=pltpu.VMEM),
+            pl.BlockSpec(memory_space=pltpu.VMEM),
+        ],
+        out_specs=(pl.BlockSpec(memory_space=pltpu.VMEM), pl.BlockSpec(memory_space=pltpu.VMEM)),
         scratch_shapes=[
             pltpu.VMEM((n, 2, share, 128), F32),
             pltpu.VMEM((share, 128), F32),
             pltpu.SemaphoreType.DMA((2, n)),
             pltpu.SemaphoreType.DMA((2, n)),
+            pltpu.VMEM((KERNELS, Q, 2 * BAND), BF16),
+            pltpu.VMEM((BAND // 128, R * count, 128), F32),
+            pltpu.VMEM((Q * count, R), F32),
         ],
-        compiler_params=pltpu.CompilerParams(collective_id=0, has_side_effects=True),
+        compiler_params=pltpu.CompilerParams(
+            collective_id=0, has_side_effects=True, vmem_limit_bytes=40 * 2**20
+        ),
         name="column_means",
-    )(part)
-    return mean.reshape(-1)
+    )(part, template_kernel_index, table, templates)
+    return mean.reshape(-1), x
 
 
 def gather_kernel(chunks, ready_ref, x_ref, acc_ref, held, send_sem, recv_sem):
@@ -259,6 +307,7 @@
     up, down = blk(z + 1, y, c), blk(z - 1, y, c)
     beside, twin = blk(z, 1 - y, c), blk(z, y, 1 - c)
 
+    middle = (z == 1) | (z == 2)
     barrier = pltpu.get_barrier_semaphore()
 
     def greet(to):
@@ -299,7 +348,8 @@
                 else:
                     one.start()
 
-            act(8 + zs, beside)
+            skip = (zs == 3 * (1 - z % 2)) & (middle | (k % 2 == 1))
+            pl.when(jnp.logical_not(skip))(lambda: act(8 + zs, beside))
             if sign > 0 or h == 0:
                 pl.when(z < planes - 1)(lambda: act(zs, up))
             if sign < 0 or h == 0:
@@ -317,10 +367,14 @@
 
         def go():
             one = copy(source, k, 16 + zs, twin)
+            along = copy(source, k, 20, jnp.where(z % 2 == 0, up, down))
+            passes = (zs == 3 * (z % 2)) & (jnp.logical_not(middle) | (k % 2 == 1))
             if finish:
                 one.wait_send()
+                pl.when(passes)(lambda: along.wait_send())
             else:
                 one.wait_recv()
+                pl.when(passes)(lambda: along.start())
                 one.start()
 
         if h == 0:
@@ -361,11 +415,11 @@
         for m in range(LAGS * count // tile):
             one_tile(m, 0)
 
-    lag = planes + 1
+    lag = planes + 1 + AHEAD
 
     def step(s, _):
-        each_hop(z_part, lambda h: s - h, False)
-        each_hop(y_part, lambda h: s - h - 1, False)
+        each_hop(z_part, lambda h: s - h - (AHEAD if h > 0 else 0), False)
+        each_hop(y_part, lambda h: s - h - 1 - AHEAD, False)
         pl.when(s >= lag)(lambda: product(s - lag))
         return 0
 
@@ -382,7 +436,7 @@
 def gather_correlate(x, ready):
     rows = ready.shape[1]
     count = x.shape[0] // (Q + LAGS)
-    chunks = 8
+    chunks = CHUNKS
     return pl.pallas_call(
         functools.partial(gather_kernel, chunks),
         out_shape=jax.ShapeDtypeStruct((LAGS * count, 16 * rows), F32),
@@ -390,7 +444,7 @@
         out_specs=pl.BlockSpec(memory_space=pltpu.VMEM),
         scratch_shapes=[
             pltpu.VMEM((16, Q, rows, R), BF16),
-            pltpu.SemaphoreType.DMA((20, chunks)),
+            pltpu.SemaphoreType.DMA((21, chunks)),
             pltpu.SemaphoreType.DMA((16, chunks)),
         ],
         compiler_params=pltpu.CompilerParams(
@@ -432,14 +486,16 @@
 ):
     rows = observed.shape[0]
     ring = devices == 16 and rows % 16 == 0
-    x = shape_templates(templates, template_kernel_index, line_spread_table)
     good = good_pixel_mask > 0
     flux = jnp.where(good, observed, 0).astype(F32)
     present = (flux > 0).astype(F32)
     sums, counts = jnp.sum(flux, axis=0), jnp.sum(present, axis=0)
     if ring:
-        mean = column_means(sums, counts, devices)
+        mean, x = column_means(
+            sums, counts, devices, templates, template_kernel_index, line_spread_table
+        )
     else:
+        x = shape_templates(templates, template_kernel_index, line_spread_table)
         sums = lax.psum(jnp.stack([sums, counts]), "blk")
         mean = sums[0] / jnp.maximum(sums[1], 1.0)
     resid = present * (flux - mean[None, :])

time: 87.7 us -> 72.5 us (0.83)
  Pallas kernels: 81.3 us -> 68.4 us
  other arithmetic: 4.79 us -> 2.45 us
    pallas_call x1, Pallas kernels: 57.6 us -> 50 us  [gather_correlate(): pl.pallas_call(functools.partial(gather_kernel, chunks), out_shape=jax.Sh...]
    pallas_call x2 -> x1, Pallas kernels: 21.8 us -> 16.6 us  [column_means(): pl.pallas_call(functools.partial(mean_kernel, n), out_shape=(jax.ShapeDty...]
where the time goes in v2:
time: 72.5 us; the launch traced here: 72.4 us
  Pallas kernels  68.4 us (94%)
  other arithmetic  2.45 us (3%)
  local copies, waits for them, and re-layouts  1.39 us (2%)
    pallas_call x1, Pallas kernels, gather_correlate(): pl.pallas_call(functools.partial(gather_kernel, chunks), out_shape=jax.Sh...  50 us
    pallas_call x1, Pallas kernels, column_means(): pl.pallas_call(functools.partial(mean_kernel, n), out_shape=(jax.ShapeDty...  16.6 us
    pallas_call x1, Pallas kernels, place(): pl.pallas_call(place_kernel, out_shape=jax.ShapeDtypeStruct((total_rows,...  1.87 us
    reduce_sum x1, other arithmetic, shards(): sums, counts = (jnp.sum(flux, axis=0), jnp.sum(present, axis=0))  1.86 us

profile of v2, /device:TPU:0, one launch (start us, length us, event | category | flops | bytes accessed | tf_op | source)
XLA Modules:
  0.0 72.4 jit_solution(8590255149106299781)
XLA Ops:
  0.0 0.0 copy-start.2
  0.0 0.0 copy-start
  0.0 0.8 %pad.4.table_ref = f32[8,640]{1,0:T(8,128)S(1)} pad(f32[8,97]{1,0:T(8,128)} %param.10, f32[]{:T(128)} %constant.12.clone.1), padding=0_0x0_543 | pad | bytes 23588 | tf_op jit(solution)/shard_map/jit(_pad)/pad | solution.py:264
  0.8 1.9 %convert_reduce_fusion = (f32[16384]{0:T(1024)S(1)}, f32[16384]{0:T(1024)S(1)}, bf16[16,16384]{1,0:T(8,128)(2,1)S(1)}) fusion(bf16[16,16384]{1,0:T(8,128)(2,1)} %param.6, s32[16,16384]{1,0:T(8,128)} %param.7), kind=kLoop, calls=%fused_computation.1 | loop fusion | flops 1802240 | bytes 2228224 | tf_op jit(solution)/shard_map/reduce_sum | solution.py:492
  2.7 0.0 copy-done.2
  2.7 0.0 copy-done
  2.7 16.6 %column_means.1 = (f32[16,8,128]{2,1,0:T(8,128)S(1)}, bf16[3072,128]{1,0:T(8,128)(2,1)S(1)}) custom-call(f32[16,2,8,128]{3,2,1,0:T(8,128)S(1)} %pad_maximum_fusion.part_ref, s32[16]{0:T(128)S(1)} %copy-done.2, f32[8,640]{1,0:T(8,128)S(1)} %pad.4.table_ref, bf16[16,65632]{1,0:T(8,128)(2,1)S(1)} %copy-done), custom_call_target="tpu_custom_call" | custom-call | tf_op jit(solution)/shard_map/column_means/pallas_call | solution.py:265
  19.3 0.3 fusion.5
  19.7 0.3 fusion.7
  19.9 0.0 copy-start.1
  19.9 0.1 copy.8
  20.0 0.4 copy.7
  20.5 50.0 %gather_correlate.1.acc_ref = f32[1024,256]{1,0:T(8,128)S(1)} custom-call(bf16[128,16,128]{2,1,0:T(8,128)(2,1)S(1)} %bitcast.8, bf16[3072,128]{1,0:T(8,128)(2,1)S(1)} %get-tuple-element.8.x_ref), custom_call_target="tpu_custom_call" | custom-call | tf_op jit(solution)/shard_map/gather_correlate/pallas_call | solution.py:440
  70.5 0.0 copy-done.1
  70.5 1.9 %place.1 = f32[256,1024]{1,0:T(8,128)} custom-call(s32[1,256]{1,0:T(1,128)S(1)} %bitcast.11, f32[1024,256]{1,0:T(8,128)S(1)} %gather_correlate.1.acc_ref), custom_call_target="tpu_custom_call" | custom-call | tf_op jit(solution)/shard_map/place/pallas_call | solution.py:467
  (2 shorter events, 0.0 us)
Async XLA Ops:
  0.0 2.7 %copy-start.2 = (s32[16]{0:T(128)S(1)}, s32[16]{0:T(128)}, u32[]{:S(2)}) copy-start(s32[16]{0:T(128)} %index_ref.1) | copy-start | bytes 196
  0.0 2.7 %copy-start = (bf16[16,65632]{1,0:T(8,128)(2,1)S(1)}, bf16[16,65632]{1,0:T(8,128)(2,1)}, u32[]{:S(2)}) copy-start(bf16[16,65632]{1,0:T(8,128)(2,1)} %templates_ref.1) | copy-start | bytes 6300676
  19.9 50.6 %copy-start.1 = (s32[256]{0:T(256)S(1)}, s32[256]{0:T(256)}, u32[]{:S(2)}) copy-start(s32[256]{0:T(256)} %param.11) | copy-start | bytes 3076

commit v3 on v2

--- a/solution.py
+++ b/solution.py
@@ -33,7 +33,10 @@
 def spread_templates(table_ref, templates_ref, bands, chunks):
     count = templates_ref.shape[0]
     for k in range(KERNELS):
-        row = jnp.broadcast_to(table_ref[k : k + 1, :], (Q, BAND))
+        row = jnp.concatenate(
+            [table_ref[k : k + 1, :], jnp.zeros((1, BAND - TAPS), F32)], axis=1
+        )
+        row = jnp.broadcast_to(row, (Q, BAND))
         band = pltpu.roll(row, 0, 1, stride=4, stride_axis=0)
         high = band.astype(BF16)
         bands[k, :, :BAND] = high
@@ -85,7 +88,6 @@
 
 def shape_templates(templates, template_kernel_index, line_spread_table):
     count = templates.shape[0]
-    table = jnp.pad(line_spread_table, ((0, 0), (0, BAND - TAPS)))
     return pl.pallas_call(
         template_kernel,
         out_shape=jax.ShapeDtypeStruct(((Q + LAGS) * count, R), BF16),
@@ -105,7 +107,7 @@
             flops=2 * count * Q * R * 2 * BAND, bytes_accessed=6 * 2**20, transcendentals=0
         ),
         name="shape_templates",
-    )(template_kernel_index, table, templates)
+    )(template_kernel_index, line_spread_table, templates)
 
 
 def place_rows(rows_ref, acc, out_ref, count):
@@ -261,7 +263,6 @@
     part = jnp.stack([sums.reshape(n, -1, 128), counts.reshape(n, -1, 128)], axis=1)
     share = part.shape[2]
     count = templates.shape[0]
-    table = jnp.pad(line_spread_table, ((0, 0), (0, BAND - TAPS)))
     mean, x = pl.pallas_call(
         functools.partial(mean_kernel, n),
         out_shape=(
@@ -288,7 +289,7 @@
             collective_id=0, has_side_effects=True, vmem_limit_bytes=40 * 2**20
         ),
         name="column_means",
-    )(part, template_kernel_index, table, templates)
+    )(part, template_kernel_index, line_spread_table, templates)
     return mean.reshape(-1), x
 
 
@@ -348,12 +349,12 @@
                 else:
                     one.start()
 
-            skip = (zs == 3 * (1 - z % 2)) & (middle | (k % 2 == 1))
-            pl.when(jnp.logical_not(skip))(lambda: act(8 + zs, beside))
             if sign > 0 or h == 0:
                 pl.when(z < planes - 1)(lambda: act(zs, up))
             if sign < 0 or h == 0:
                 pl.when(z > 0)(lambda: act(4 + zs, down))
+            skip = (zs == 3 * (1 - z % 2)) & (middle | (k % 2 == 1))
+            pl.when(jnp.logical_not(skip))(lambda: act(8 + zs, beside))
             act(12 + zs, twin)
 
         if h == 0:

time: 72.5 us -> 71.8 us (level)
  local copies, waits for them, and re-layouts: 1.39 us -> 0.6 us
    pad x1 -> x0, local copies, waits for them, and re-layouts: 0.84 us -> none  [column_means(): table = jnp.pad(line_spread_table, ((0, 0), (0, BAND - TAPS)))]
where the time goes in v3:
time: 71.8 us; the launch traced here: 71.7 us
  Pallas kernels  68.4 us (95%)
  other arithmetic  2.6 us (4%)
    pallas_call x1, Pallas kernels, gather_correlate(): pl.pallas_call(functools.partial(gather_kernel, chunks), out_shape=jax.Sh...  50 us
    pallas_call x1, Pallas kernels, column_means(): pl.pallas_call(functools.partial(mean_kernel, n), out_shape=(jax.ShapeDty...  16.6 us
    reduce_sum x1, other arithmetic, shards(): sums, counts = (jnp.sum(flux, axis=0), jnp.sum(present, axis=0))  2 us
    pallas_call x1, Pallas kernels, place(): pl.pallas_call(place_kernel, out_shape=jax.ShapeDtypeStruct((total_rows,...  1.86 us

profile of v3, /device:TPU:0, one launch (start us, length us, event | category | flops | bytes accessed | tf_op | source)
XLA Modules:
  0.0 71.7 jit_solution(1949928076680299085)
XLA Ops:
  0.0 0.0 copy-start.1
  0.0 0.0 copy-start.3
  0.0 0.0 copy-start
  0.0 2.0 %convert_reduce_fusion = (f32[16384]{0:T(1024)S(1)}, f32[16384]{0:T(1024)S(1)}, bf16[16,16384]{1,0:T(8,128)(2,1)S(1)}) fusion(bf16[16,16384]{1,0:T(8,128)(2,1)} %param.6, s32[16,16384]{1,0:T(8,128)} %param.7), kind=kLoop, calls=%fused_computation.1 | loop fusion | flops 1802240 | bytes 2228224 | tf_op jit(solution)/shard_map/reduce_sum | solution.py:493
  2.0 0.0 copy-done.1
  2.0 0.0 copy-done.3
  2.0 0.0 copy-done
  2.1 16.6 %column_means.1 = (f32[16,8,128]{2,1,0:T(8,128)S(1)}, bf16[3072,128]{1,0:T(8,128)(2,1)S(1)}) custom-call(f32[16,2,8,128]{3,2,1,0:T(8,128)S(1)} %pad_maximum_fusion.part_ref, s32[16]{0:T(128)S(1)} %copy-done.3, f32[8,97]{1,0:T(8,128)S(1)} %copy-done.1, bf16[16,65632]{1,0:T(8,128)(2,1)S(1)} %copy-done), custom_call_target="tpu_custom_call" | custom-call | tf_op jit(solution)/shard_map/column_means/pallas_call | solution.py:266
  18.7 0.3 fusion.5
  19.0 0.3 fusion.7
  19.3 0.0 copy-start.2
  19.3 0.1 copy.8
  19.4 0.4 copy.7
  19.8 50.0 %gather_correlate.1.acc_ref = f32[1024,256]{1,0:T(8,128)S(1)} custom-call(bf16[128,16,128]{2,1,0:T(8,128)(2,1)S(1)} %bitcast.8, bf16[3072,128]{1,0:T(8,128)(2,1)S(1)} %get-tuple-element.8.x_ref), custom_call_target="tpu_custom_call" | custom-call | tf_op jit(solution)/shard_map/gather_correlate/pallas_call | solution.py:441
  69.8 0.0 copy-done.2
  69.8 1.9 %place.1 = f32[256,1024]{1,0:T(8,128)} custom-call(s32[1,256]{1,0:T(1,128)S(1)} %bitcast.11, f32[1024,256]{1,0:T(8,128)S(1)} %gather_correlate.1.acc_ref), custom_call_target="tpu_custom_call" | custom-call | tf_op jit(solution)/shard_map/place/pallas_call | solution.py:468
  (2 shorter events, 0.0 us)
Async XLA Ops:
  0.0 2.0 %copy-start.1 = (f32[8,97]{1,0:T(8,128)S(1)}, f32[8,97]{1,0:T(8,128)}, u32[]{:S(2)}) copy-start(f32[8,97]{1,0:T(8,128)} %table_ref.1) | copy-start | bytes 9316
  0.0 2.0 %copy-start.3 = (s32[16]{0:T(128)S(1)}, s32[16]{0:T(128)}, u32[]{:S(2)}) copy-start(s32[16]{0:T(128)} %index_ref.1) | copy-start | bytes 196
  0.0 2.1 %copy-start = (bf16[16,65632]{1,0:T(8,128)(2,1)S(1)}, bf16[16,65632]{1,0:T(8,128)(2,1)}, u32[]{:S(2)}) copy-start(bf16[16,65632]{1,0:T(8,128)(2,1)} %templates_ref.1) | copy-start | bytes 6300676
  19.3 50.6 %copy-start.2 = (s32[256]{0:T(256)S(1)}, s32[256]{0:T(256)}, u32[]{:S(2)}) copy-start(s32[256]{0:T(256)} %param.11) | copy-start | bytes 3076
